TPU v7x, 32 devices: a whole 2x2x4 slice. The times are simulated.
32 devices in a mesh: groups: 2 (over x), wide: 16 (over z, y, core).
Axes of the slice: x: 2, y: 2, z: 4, core: 2. Of those that a mesh axis runs over, the one named last changes fastest.
Arguments:
- hidden_in: bfloat16 [512, 16384], P('groups', 'wide'), parts along dimension 0, may hold values from -100 to 100
- query_values: bfloat16 [16384, 8192], P('wide'), may hold values from -0.046875 to 0.046875
- query_scales: float32 [1024, 8192], P('wide'), may hold values from 0.5 to 2
- pair_values: bfloat16 [16384, 1024], P('wide'), may hold values from -0.046875 to 0.046875
- pair_scales: float32 [1024, 1024], P('wide'), may hold values from 0.5 to 2
- output_values: bfloat16 [8192, 16384], P('wide'), may hold values from -0.0625 to 0.0625
- output_scales: float32 [512, 16384], P('wide'), may hold values from 0.5 to 2
- tensor_scales: float32 [4], replicated, may hold values from 0.6 to 1.6
Outputs:
- attended_out: bfloat16 [512, 16384], P('groups', 'wide'), parts along dimension 0
There are 2 independent parts, one for each index of `groups`. A program takes and returns all parts, laid end to end along the dimension named above; an argument that names none is the same for every part. Nothing has to cross between parts.
All inputs are finite; a program needn't handle non-finite values.
Results may differ from a plain program's by a relative error of at most 0.012.
The roundings to bfloat16 on the way count: a program that leaves them out, or rounds other values in their place, can miss the bound.
Values may be sent and summed in bfloat16 or wider, within the bound.
A program may use at most 192 MiB of HBM per device.

v0:
```python
import math

import jax
import jax.numpy as jnp
from jax import lax
from jax.sharding import PartitionSpec as P

HEADS = 64
KV_HEADS = 4
HEAD_DIM = 128


def dequantize(values, scales):
    expanded = jnp.repeat(scales, 16, axis=0)
    return (values.astype(jnp.float32) * expanded).astype(jnp.bfloat16)


def rotary_angles(head_dim, length):
    half = head_dim // 2
    freq = jnp.exp(jnp.arange(half, dtype=jnp.float32) * (-2.0 * math.log(500000.0) / head_dim))
    position = jnp.arange(length, dtype=jnp.float32)
    return position[:, None] * freq[None, :]


def rotate_rows(field):
    half = field.shape[1] // 2
    angle = rotary_angles(field.shape[1], field.shape[2])
    cosine = jnp.cos(angle).T[None]
    sine = jnp.sin(angle).T[None]
    lower = field[:, :half]
    upper = field[:, half:]
    return jnp.concatenate([lower * cosine - upper * sine, upper * cosine + lower * sine], axis=1)


def features_term(weight, activ):
    return lax.dot_general(
        weight, activ, (((0,), (1,)), ((), ())), preferred_element_type=jnp.float32
    )


def on_device(
    hidden_in,
    query_values,
    query_scales,
    pair_values,
    pair_scales,
    output_values,
    output_scales,
    tensor_scales,
):
    devices = lax.axis_size("wide")
    position = lax.axis_index("wide")
    tok_count = hidden_in.shape[0]
    query_weight = dequantize(query_values, query_scales)
    pair_weight = dequantize(pair_values, pair_scales)
    query_rows = query_values.shape[1] // devices
    query_t = (
        lax.psum_scatter(
            features_term(query_weight, hidden_in), "wide", scatter_dimension=0, tiled=True
        )
        * tensor_scales[0]
    )
    local_heads = query_rows // HEAD_DIM
    query_t = rotate_rows(query_t.reshape(local_heads, HEAD_DIM, tok_count)).astype(jnp.bfloat16)
    pair_part = lax.psum_scatter(
        features_term(pair_weight, hidden_in), "wide", scatter_dimension=0, tiled=True
    )
    pair_all = lax.all_gather(pair_part, "wide", axis=0, tiled=True)
    half_width = pair_all.shape[0] // 2
    key_head = position * local_heads // (HEADS // KV_HEADS)
    key_rows = (
        lax.dynamic_slice_in_dim(pair_all[:half_width], key_head * HEAD_DIM, HEAD_DIM, 0)
        * tensor_scales[1]
    )
    value_rows = (
        lax.dynamic_slice_in_dim(pair_all[half_width:], key_head * HEAD_DIM, HEAD_DIM, 0)
        * tensor_scales[2]
    )
    key_rows = rotate_rows(key_rows[None])[0].astype(jnp.bfloat16)
    value_rows = value_rows.astype(jnp.bfloat16)
    scores = jnp.einsum(
        "hdq,dk->hqk", query_t, key_rows, preferred_element_type=jnp.float32
    ) / math.sqrt(HEAD_DIM)
    causal = jnp.arange(tok_count)[:, None] >= jnp.arange(tok_count)[None, :]
    scores = jnp.where(causal[None], scores, -1e30)
    top = jnp.max(scores, axis=-1, keepdims=True)
    expo = jnp.exp(scores - top)
    weights = (expo / jnp.sum(expo, axis=-1, keepdims=True)).astype(jnp.bfloat16)
    mixed = jnp.einsum("hqk,dk->qhd", weights, value_rows, preferred_element_type=jnp.float32)
    mixed = mixed.reshape(tok_count, local_heads * HEAD_DIM).astype(jnp.bfloat16)
    output_weight = dequantize(output_values, output_scales)
    summed = (
        lax.psum_scatter(
            features_term(output_weight, mixed), "wide", scatter_dimension=0, tiled=True
        )
        * tensor_scales[3]
    )
    return summed.astype(jnp.bfloat16).T


def solution(mesh):
    in_specs = (
        P("groups", "wide"),
        P("wide", None),
        P("wide", None),
        P("wide", None),
        P("wide", None),
        P("wide", None),
        P("wide", None),
        P(),
    )
    out_specs = P("groups", "wide")
    return jax.shard_map(
        on_device, mesh=mesh, in_specs=in_specs, out_specs=out_specs, check_vma=False
    )
```

profile of v0, /device:TPU:10, one launch (start us, length us, event | category | flops | bytes accessed | tf_op | source)
XLA Modules:
  0.0 423.6 jit_solution(835365229653997907)
XLA Ops:
  6.5 0.0 copy-start
  6.5 0.0 reduce-scatter.4.cloned.1.call-start
  6.5 2.2 fusion.3
  8.8 0.0 copy-done
  8.8 1.7 fusion.32
  10.5 0.0 reduce-scatter.4.cloned.1.call-update
  10.5 0.0 all-gather.2.cloned.1.call-start
  10.6 58.8 %reduce-scatter.4.cloned.1.call-done = f32[64,256]{1,0:T(8,128)} async-done(((f32[1024,256]{1,0:T(8,128)}), f32[64,256]{1,0:T(8,128)}) %reduce-scatter.4.cloned.1.call-update) | async-done | bytes 65552 | tf_op jit(solution)/shard_map/reduce_scatter | solution.py:65
  69.4 0.0 all-gather.2.cloned.1.call-update
  69.4 0.0 reduce-scatter.6.cloned.1.call-start
  69.5 10.1 %fusion.1 = bf16[1024,8192]{1,0:T(8,128)(2,1)S(1)} fusion(bf16[1024,8192]{1,0:T(8,128)(2,1)} %param.9, f32[64,8192]{1,0:T(8,128)} %param.10), kind=kLoop, calls=%fused_computation.2 | loop fusion | flops 25165824 | bytes 35651584 | tf_op jit(solution)/shard_map/convert_element_type | solution.py:15
  79.6 0.0 copy-start.2
  79.6 6.9 %fusion.33 = f32[8192,256]{1,0:T(8,128)} fusion(bf16[1024,8192]{1,0:T(8,128)(2,1)S(1)} %fusion.1, bf16[256,1024]{1,0:T(8,128)(2,1)S(1)} %copy-done), kind=kOutput, calls=%fused_computation.46 | convolution fusion | flops 4294967296 | bytes 25690112 | tf_op jit(solution)/shard_map/dot_general | solution.py:36
  86.5 0.0 reduce-scatter.6.cloned.1.call-update
  86.5 0.2 reduce-scatter.8.cloned.1.call-start
  86.8 0.0 copy-done.2
  86.8 0.0 copy-start.3
  86.8 15.3 %fusion.2 = bf16[512,16384]{1,0:T(8,128)(2,1)} fusion(bf16[512,16384]{1,0:T(8,128)(2,1)} %param.13, f32[32,16384]{1,0:T(8,128)S(1)} %copy-done.2), kind=kLoop, calls=%fused_computation.4 | loop fusion | flops 25165824 | bytes 35651584 | tf_op jit(solution)/shard_map/convert_element_type | solution.py:15
  102.1 0.0 copy-done.3
  102.1 0.7 fusion.28
  102.8 0.3 fusion.18
  103.1 4.8 %all-gather.2.cloned.1.call-done = f32[1024,256]{1,0:T(8,128)} async-done(((f32[64,256]{1,0:T(8,128)}), f32[1024,256]{1,0:T(8,128)}) %all-gather.2.cloned.1.call-update) | async-done | bytes 1048592 | tf_op jit(solution)/shard_map/all_gather | solution.py:68
  107.9 1.3 fusion.27
  109.2 0.6 multiply_bitcast_fusion
  109.9 0.3 subtract_convert_fusion.1
  110.2 107.1 %reduce-scatter.6.cloned.1.call-done = f32[512,256]{1,0:T(8,128)} async-done(((f32[8192,256]{1,0:T(8,128)}), f32[512,256]{1,0:T(8,128)}) %reduce-scatter.6.cloned.1.call-update) | async-done | bytes 524304 | tf_op jit(solution)/shard_map/reduce_scatter | solution.py:58
  217.3 1.7 broadcast_multiply_fusion
  219.0 0.1 subtract_convert_fusion
  219.0 0.5 fusion.29
  219.6 0.3 fusion.6
  219.9 1.1 convolution_convert_fusion
  221.0 0.0 copy-start.1
  221.0 16.1 %fusion.34 = f32[16384,256]{1,0:T(8,128)} fusion(bf16[512,16384]{1,0:T(8,128)(2,1)} %fusion.2, bf16[256,512]{0,1:T(8,128)(2,1)S(1)} %bitcast.44), kind=kOutput, calls=%fused_computation.47 | convolution fusion | flops 4294967296 | bytes 33816576 | tf_op jit(solution)/shard_map/dot_general | solution.py:36
  237.1 0.0 reduce-scatter.8.cloned.1.call-update
  237.2 176.9 %reduce-scatter.8.cloned.1.call-done = f32[1024,256]{1,0:T(8,128)} async-done(((f32[16384,256]{1,0:T(8,128)}), f32[1024,256]{1,0:T(8,128)}) %reduce-scatter.8.cloned.1.call-update) | async-done | bytes 1048592 | tf_op jit(solution)/shard_map/reduce_scatter | solution.py:93
  414.1 2.0 fusion.7
  416.0 1.0 copy.11
  417.0 0.0 copy-done.1
  (2 shorter events, 0.0 us)
Async XLA Ops:
  6.5 2.2 copy-start
  6.5 62.9 %reduce-scatter.4.cloned.1.call-start = ((), (), s32[]{:S(2)}) async-start(), calls=%async_computation.3 | async-start | bytes 1114112 | tf_op jit(solution)/shard_map/reduce_scatter | solution.py:65
  10.5 97.4 %all-gather.2.cloned.1.call-start = ((), (), s32[]{:S(2)}) async-start(), calls=%async_computation.4 | async-start | bytes 1114112 | tf_op jit(solution)/shard_map/all_gather | solution.py:68
  69.4 147.8 %reduce-scatter.6.cloned.1.call-start = ((), (), s32[]{:S(2)}) async-start(), calls=%async_computation.5 | async-start | bytes 8912896 | tf_op jit(solution)/shard_map/reduce_scatter | solution.py:58
  79.6 7.2 %copy-start.2 = (f32[32,16384]{1,0:T(8,128)S(1)}, f32[32,16384]{1,0:T(8,128)}, u32[]{:S(2)}) copy-start(f32[32,16384]{1,0:T(8,128)} %param.14) | copy-start | bytes 6291460
  86.5 327.5 %reduce-scatter.8.cloned.1.call-start = ((), (), s32[]{:S(2)}) async-start(), calls=%async_computation.6 | async-start | bytes 17825792 | tf_op jit(solution)/shard_map/reduce_scatter | solution.py:93
  86.8 15.3 %copy-start.3 = (f32[4]{0:T(128)S(1)}, f32[4]{0:T(128)}, u32[]{:S(2)}) copy-start(f32[4]{0:T(128)} %param.15) | copy-start | bytes 52
  221.0 196.0 %copy-start.1 = (bf16[256,1024]{1,0:T(8,128)(2,1)S(1)}, bf16[256,1024]{1,0:T(8,128)(2,1)}, u32[]{:S(2)}) copy-start(bf16[256,1024]{1,0:T(8,128)(2,1)} %param.8) | copy-start | bytes 1572868
Sparse Core Ops, SparseCore 0:
  11.0 58.3 reduce-scatter.3
  71.8 36.1 all-gather.1
  112.6 104.6 reduce-scatter.5
  237.3 176.7 reduce-scatter.7
where the time goes:
time: 427 us; the launch traced here: 424 us
  waiting for transfers between devices  348 us (81%)
  other arithmetic  32.6 us (8%)
  matrix products  26.7 us (6%)
  between operations  13.3 us (3%)
    reduce_scatter x1, waiting for transfers between devices, on_device(): lax.psum_scatter(features_term(output_weight, mixed), 'wide', scatter_dim...  177 us
    reduce_scatter x1, waiting for transfers between devices, on_device(): lax.psum_scatter(features_term(query_weight, hidden_in), 'wide', scatter_...  107 us
    reduce_scatter x1, waiting for transfers between devices, on_device(): lax.psum_scatter(features_term(pair_weight, hidden_in), 'wide', scatter_d...  58.8 us
    convert_element_type x3, other arithmetic, dequantize(): return (values.astype(jnp.float32) * expanded).astype(jnp.bfloat16)  27.6 us
    dot_general x3, matrix products, features_term(): lax.dot_general(weight, activ, (((0,), (1,)), ((), ())), preferred_elemen...  24.8 us
  transfers between devices with their start and end apart: 4, of which 4 were waited for; matrix products, arithmetic and copies ran while one was open for 8% of the time, Pallas kernels for 0%

commit v1 on v0

v1 whole, which is shorter than its diff:
```python
import functools
import math

import jax
import jax.numpy as jnp
import numpy as np
from jax import lax
from jax.experimental import pallas as pl
from jax.experimental.pallas import tpu as pltpu
from jax.sharding import PartitionSpec as P

HEADS = 64
KV_HEADS = 4
HEAD_DIM = 128
MESH = pl.DeviceIdType.MESH
F32 = jnp.float32
BF16 = jnp.bfloat16
TILES = 3
SIBLING_SLOTS = 3


def div(a, b):
    return lax.div(a, jnp.int32(b)) if not isinstance(a, int) else a // b


def rem(a, b):
    return lax.rem(a, jnp.int32(b)) if not isinstance(a, int) else a % b


def at_least_zero(a, big):
    return div(a + big, big)


def line_order(z, length, j):
    high = div(2 * z, length)
    low = z + high * (length - 1 - 2 * z)
    far = length - 1 - 2 * low
    m = j - far
    later = at_least_zero(m, 4 * length)
    m = m * later
    odd = rem(m, 2)
    near = div(m, 2) * (1 - 2 * odd) + odd * 2 * low
    place = later * near + (1 - later) * (length - 1 - j)
    return place + high * (length - 1 - 2 * place)


def rotary_tables(length):
    half = HEAD_DIM // 2
    freq = np.exp(np.arange(half, dtype=np.float32) * np.float32(-2.0 * math.log(500000.0) / HEAD_DIM))
    angle = np.arange(length, dtype=np.float32)[:, None] * freq.astype(np.float32)[None, :]
    angle = angle.astype(np.float64)
    cosine, sine = np.cos(angle), np.sin(angle)
    return (
        np.concatenate([cosine, cosine], axis=1).astype(np.float32),
        np.concatenate([-sine, sine], axis=1).astype(np.float32),
    )


def block_kernel(
    devices, length, rows_y,
    hidden, query_values, query_scales, pair_values, pair_scales, output_values, output_scales,
    tensor_scales, cosine, sine,
    out,
    tiles, tile_scales, tile_sem, tile_scales_sem, dequantized, acc,
    pair_buf, pair_scales_buf, pair_sem, kv_part,
    out_weight, out_scales, out_sem,
    a_send, a_recv, a_ysend, a_yrecv, a_own, a_up, a_down,
    a_ss, a_sr, a_ys, a_yr, a_zs, a_ur, a_dr,
    b_send, b_recv, b_ysend, b_yrecv, b_own, b_up, b_down,
    b_ss, b_sr, b_ys, b_yr, b_zs, b_ur, b_dr,
    kv_all, kv_send_sem, kv_recv_sem, keys, values, mixed,
):
    tokens, depth = hidden.shape
    block_a = query_values.shape[1] // devices
    block_b = output_values.shape[1] // devices
    depth_b = output_values.shape[0]
    sharers = devices // KV_HEADS
    half = pair_values.shape[1] // 2
    share_rows = tokens // sharers
    fold = block_a // (2 * HEAD_DIM)
    extra = share_rows // fold
    cells = length * rows_y
    steps = 2 * cells

    me = lax.axis_index("wide")
    core = rem(me, 2)
    y = rem(div(me, 2), rows_y)
    z = div(me, 2 * rows_y)
    share = rem(me, sharers)
    sibling = me + 1 - 2 * core
    across = me + 2 * (1 - 2 * y) if rows_y == 2 else me
    stride = 2 * rows_y

    def cell_device(k, owner_core):
        zt = line_order(z, length, rem(k, length))
        yt = rem(y + 1 + div(k, length), 2) if rows_y == 2 else y
        return (zt * rows_y + yt) * 2 + owner_core

    def step_info(t):
        odd = rem(t, 2)
        first = div(steps - t, steps)
        last = div(t + 1, steps)
        for_sibling = first + odd * (1 - last)
        k = div(t - 1 + 2 * for_sibling, 2)
        return for_sibling, k, cell_device(k, core + for_sibling * (1 - 2 * core))

    def tile_copies(t):
        _, _, dest = step_info(t)
        slot = rem(t, TILES)
        columns = pl.ds(pl.multiple_of(dest * block_a, block_a), block_a)
        return (
            pltpu.make_async_copy(query_values.at[:, columns], tiles.at[slot], tile_sem.at[slot]),
            pltpu.make_async_copy(query_scales.at[:, columns], tile_scales.at[slot], tile_scales_sem.at[slot]),
        )

    pair_copies = (
        pltpu.make_async_copy(pair_values, pair_buf, pair_sem.at[0]),
        pltpu.make_async_copy(pair_scales, pair_scales_buf, pair_sem.at[1]),
    )
    part_b = output_values.shape[1] // length

    def out_copies(j):
        columns = pl.ds(pl.multiple_of(j * part_b, part_b), part_b)
        return (
            pltpu.make_async_copy(output_values.at[:, columns], out_weight.at[:, columns], out_sem.at[0, j]),
            pltpu.make_async_copy(output_scales.at[:, columns], out_scales.at[:, columns], out_sem.at[1, j]),
        )

    for copy in pair_copies:
        copy.start()
    for t in range(TILES - 1):
        for copy in tile_copies(jnp.int32(t)):
            copy.start()

    barrier = pltpu.get_barrier_semaphore()

    def greet(device):
        pl.semaphore_signal(barrier, inc=1, device_id={"wide": device}, device_id_type=MESH)

    for i in range(1, sharers):
        greet(me - share + rem(share + i, sharers))

    @pl.when(z > 0)
    def _():
        greet(me - stride)

    @pl.when(z < length - 1)
    def _():
        greet(me + stride)

    def dequantize(source, scales, target, count, column, width, wide_column):
        for r in range(count):
            rows = pl.ds(16 * r, 16)
            scaled = source[rows, pl.ds(wide_column, width)].astype(F32) * scales[pl.ds(r, 1), pl.ds(wide_column, width)]
            target[rows, pl.ds(column, width)] = scaled.astype(BF16)

    for copy in pair_copies:
        copy.wait()

    @pl.loop(0, 2 * half // 256)
    def _(i):
        column = pl.multiple_of(i * 256, 256)
        dequantize(pair_buf, pair_scales_buf, dequantized, depth // 16, 0, 256, column)
        product = jnp.dot(hidden[...], dequantized[:, :256], preferred_element_type=F32)
        part = div(i, half // 256)
        head = 2 * rem(i, half // 256)
        into = pl.ds(pl.multiple_of(part * HEAD_DIM, HEAD_DIM), HEAD_DIM)
        kv_part[head, :, into] = product[:, :HEAD_DIM]
        kv_part[head + 1, :, into] = product[:, HEAD_DIM:]

    pl.semaphore_wait(
        barrier, sharers - 1 + jnp.minimum(z, 1) + jnp.minimum(length - 1 - z, 1)
    )

    def remote(source, target, send_sem, recv_sem, device):
        return pltpu.make_async_remote_copy(
            src_ref=source, dst_ref=target, send_sem=send_sem, recv_sem=recv_sem,
            device_id={"wide": device}, device_id_type=MESH,
        )

    def reduce_scatter(multiply, rows, width, between, bufs):
        send, recv, ysend, yrecv, own, up, down, ss, sr, ys, yr, zs, ur, dr = bufs
        block = acc.at[pl.ds(0, rows), pl.ds(0, width)]

        def to_sibling(k):
            slot = rem(k, SIBLING_SLOTS)
            return remote(send.at[slot], recv.at[k], ss.at[slot], sr.at[k], sibling)

        def to_across(j):
            return remote(ysend.at[j], yrecv.at[j], ys.at[j], yr.at[j], across)

        @pl.loop(0, steps)
        def _(t):
            for_sibling, k, dest = step_info(t)
            multiply(t, dest)

            @pl.when(for_sibling == 1)
            def _():
                @pl.when(k >= SIBLING_SLOTS)
                def _():
                    to_sibling(k - SIBLING_SLOTS).wait_send()

                send[rem(k, SIBLING_SLOTS)] = block[...].astype(BF16)
                to_sibling(k).start()

            @pl.when(for_sibling == 0)
            def _():
                to_sibling(k).wait_recv()
                if rows_y == 2:
                    @pl.when(k < length)
                    def _():
                        ysend[k] = (block[...] + recv[k].astype(F32)).astype(BF16)
                        to_across(k).start()

                    @pl.when(k >= length)
                    def _():
                        own[k - length] = block[...] + recv[k].astype(F32)
                else:
                    own[k] = block[...] + recv[k].astype(F32)

        for k in range(cells - SIBLING_SLOTS, cells):
            to_sibling(k).wait_send()

        def to_up(j, zt):
            return remote(yrecv.at[j], up.at[zt], zs.at[j], ur.at[zt], me + stride)

        def to_down(j, zt):
            return remote(yrecv.at[j], down.at[zt], zs.at[j], dr.at[zt], me - stride)

        def collect(j):
            if rows_y == 2:
                to_across(j).wait_recv()
                own[j] = own[j] + yrecv[j].astype(F32)

        def from_below(j, zt):
            @pl.when(z > 0)
            def _():
                to_up(0, zt).wait_recv()
                own[j] = own[j] + up[zt].astype(F32)

        def from_above(j, zt):
            @pl.when(z < length - 1)
            def _():
                to_down(0, zt).wait_recv()
                own[j] = own[j] + down[zt].astype(F32)

        @pl.loop(0, length - 1)
        def _(j):
            between(j)
            zt = line_order(z, length, j)
            collect(j)

            @pl.when(zt > z)
            def _():
                from_below(j, zt)
                yrecv[j] = own[j].astype(BF16)
                to_up(j, zt).start()

            @pl.when(zt < z)
            def _():
                from_above(j, zt)
                yrecv[j] = own[j].astype(BF16)
                to_down(j, zt).start()

        between(length - 1)
        collect(length - 1)
        from_below(length - 1, z)
        from_above(length - 1, z)

        def settle():
            for j in range(length - 1):
                to_up(j, z).wait_send()
            if rows_y == 2:
                for j in range(length):
                    to_across(j).wait_send()

        return own.at[length - 1], settle

    def multiply_a(t, dest):
        @pl.when(t + TILES - 1 < steps)
        def _():
            for copy in tile_copies(t + TILES - 1):
                copy.start()

        for copy in tile_copies(t):
            copy.wait()
        slot = rem(t, TILES)
        dequantize(tiles.at[slot], tile_scales.at[slot], dequantized, depth // 16, 0, block_a, 0)
        acc[:tokens, :block_a] = jnp.dot(hidden[...], dequantized[:, :block_a], preferred_element_type=F32)
        head, piece = div(dest, sharers), rem(dest, sharers)
        for i in range(fold):
            first = pl.multiple_of(piece * share_rows + i * extra, extra)
            acc[tokens:tokens + extra, i * 2 * HEAD_DIM:(i + 1) * 2 * HEAD_DIM] = kv_part[head, pl.ds(first, extra), :]

        @pl.when(t == steps - TILES)
        def _():
            for j in range(length):
                for copy in out_copies(j):
                    copy.start()

    def prepare_output(j):
        for copy in out_copies(j):
            copy.wait()

        @pl.loop(0, part_b // 512)
        def _(i):
            column = pl.multiple_of(j * part_b + i * 512, 512)
            dequantize(out_weight, out_scales, out_weight, depth_b // 16, column, 512, column)

    total, settle_a = reduce_scatter(
        multiply_a, tokens + extra, block_a, prepare_output,
        (a_send, a_recv, a_ysend, a_yrecv, a_own, a_up, a_down, a_ss, a_sr, a_ys, a_yr, a_zs, a_ur, a_dr),
    )

    def to_sharer(i):
        other = rem(share + i, sharers)
        return remote(
            kv_all.at[share], kv_all.at[share], kv_send_sem.at[other], kv_recv_sem.at[share], me - share + other
        )

    def from_sharer(i):
        other = rem(share + i, sharers)
        return remote(
            kv_all.at[other], kv_all.at[other], kv_send_sem.at[other], kv_recv_sem.at[other], me - share + other
        )

    kv_all[share] = total[tokens:, :]
    for i in range(1, sharers):
        to_sharer(i).start()
    settle_a()

    def rotate(field):
        return field * cosine[...] + pltpu.roll(field, HEAD_DIM // 2, 1) * sine[...]

    local_heads = block_a // HEAD_DIM
    queries = [
        rotate(total[:tokens, h * HEAD_DIM:(h + 1) * HEAD_DIM] * tensor_scales[0]).astype(BF16)
        for h in range(local_heads)
    ]
    for i in range(1, sharers):
        from_sharer(i).wait_recv()
    for q in range(sharers):
        for i in range(fold):
            rows = slice(q * share_rows + i * extra, q * share_rows + (i + 1) * extra)
            first = i * 2 * HEAD_DIM
            keys[rows, :] = kv_all[q, :, first:first + HEAD_DIM]
            values[rows, :] = kv_all[q, :, first + HEAD_DIM:first + 2 * HEAD_DIM]
    key_rows = rotate(keys[...] * tensor_scales[1]).astype(BF16)
    value_rows = (values[...] * tensor_scales[2]).astype(BF16)
    causal = lax.broadcasted_iota(jnp.int32, (tokens, tokens), 0) >= lax.broadcasted_iota(
        jnp.int32, (tokens, tokens), 1
    )
    for h in range(local_heads):
        scores = lax.dot_general(
            queries[h], key_rows, (((1,), (1,)), ((), ())), preferred_element_type=F32
        ) / math.sqrt(HEAD_DIM)
        scores = jnp.where(causal, scores, -1e30)
        top = jnp.max(scores, axis=-1, keepdims=True)
        expo = jnp.exp(scores - top)
        weights = (expo / jnp.sum(expo, axis=-1, keepdims=True)).astype(BF16)
        mixed[:, h * HEAD_DIM:(h + 1) * HEAD_DIM] = jnp.dot(
            weights, value_rows, preferred_element_type=F32
        ).astype(BF16)
    for i in range(1, sharers):
        to_sharer(i).wait_send()

    def multiply_b(t, dest):
        columns = pl.ds(pl.multiple_of(dest * block_b, block_b), block_b)
        acc[:tokens, :block_b] = jnp.dot(mixed[...], out_weight[:, columns], preferred_element_type=F32)

    summed, settle_b = reduce_scatter(
        multiply_b, tokens, block_b, lambda j: None,
        (b_send, b_recv, b_ysend, b_yrecv, b_own, b_up, b_down, b_ss, b_sr, b_ys, b_yr, b_zs, b_ur, b_dr),
    )
    out[...] = (summed[...] * tensor_scales[3]).astype(BF16)
    settle_b()


def on_device(
    hidden_in, query_values, query_scales, pair_values, pair_scales, output_values, output_scales, tensor_scales
):
    devices = lax.axis_size("wide")
    rows_y = 2 if devices == 16 else 1
    length = devices // (2 * rows_y)
    cells = length * rows_y
    tokens, depth = hidden_in.shape
    block_a = query_values.shape[1] // devices
    block_b = output_values.shape[1] // devices
    sharers = devices // KV_HEADS
    extra = tokens // sharers // (block_a // (2 * HEAD_DIM))
    cosine, sine = rotary_tables(tokens)
    dma = pltpu.SemaphoreType.DMA

    def buffers(rows, width):
        slots_y = length if rows_y == 2 else 1
        return [
            pltpu.VMEM((SIBLING_SLOTS, rows, width), BF16),
            pltpu.VMEM((cells, rows, width), BF16),
            pltpu.VMEM((slots_y, rows, width) if rows_y == 2 else (1, 16, 128), BF16),
            pltpu.VMEM((length, rows, width), BF16),
            pltpu.VMEM((length, rows, width), F32),
            pltpu.VMEM((length, rows, width), BF16),
            pltpu.VMEM((length, rows, width), BF16),
            dma((SIBLING_SLOTS,)), dma((cells,)), dma((length,)), dma((length,)),
            dma((length,)), dma((length,)), dma((length,)),
        ]

    anywhere = pl.BlockSpec(memory_space=pl.ANY)
    vmem = pl.BlockSpec(memory_space=pltpu.VMEM)
    features = query_values.shape[1] + pair_values.shape[1]
    return pl.pallas_call(
        functools.partial(block_kernel, devices, length, rows_y),
        out_shape=jax.ShapeDtypeStruct((tokens, block_b), BF16),
        in_specs=[vmem] + [anywhere] * 6 + [pl.BlockSpec(memory_space=pltpu.SMEM), vmem, vmem],
        out_specs=vmem,
        scratch_shapes=[
            pltpu.VMEM((TILES, depth, block_a), BF16),
            pltpu.VMEM((TILES, depth // 16, block_a), F32),
            dma((TILES,)), dma((TILES,)),
            pltpu.VMEM((depth, max(block_a, 256)), BF16),
            pltpu.VMEM((tokens + extra, max(block_a, block_b)), F32),
            pltpu.VMEM(pair_values.shape, BF16),
            pltpu.VMEM(pair_scales.shape, F32),
            dma((2,)),
            pltpu.VMEM((KV_HEADS, tokens, 2 * HEAD_DIM), F32),
            pltpu.VMEM(output_values.shape, BF16),
            pltpu.VMEM(output_scales.shape, F32),
            dma((2, length)),
        ]
        + buffers(tokens + extra, block_a)
        + buffers(tokens, block_b)
        + [
            pltpu.VMEM((sharers, extra, block_a), F32),
            dma((sharers,)), dma((sharers,)),
            pltpu.VMEM((tokens, HEAD_DIM), F32),
            pltpu.VMEM((tokens, HEAD_DIM), F32),
            pltpu.VMEM((tokens, block_a), BF16),
        ],
        compiler_params=pltpu.CompilerParams(
            collective_id=0, has_side_effects=True, vmem_limit_bytes=63 * 1024 * 1024
        ),
        cost_estimate=pl.CostEstimate(
            flops=2 * tokens * (depth * features + output_values.size),
            bytes_accessed=2 * (query_values.size + pair_values.size + output_values.size),
            transcendentals=tokens * tokens * (block_a // HEAD_DIM),
        ),
    )(
        hidden_in, query_values, query_scales, pair_values, pair_scales, output_values, output_scales,
        tensor_scales, jnp.asarray(cosine), jnp.asarray(sine),
    )


def solution(mesh):
    in_specs = (P("groups", "wide"),) + (P("wide", None),) * 6 + (P(),)
    return jax.shard_map(
        on_device, mesh=mesh, in_specs=in_specs, out_specs=P("groups", "wide"), check_vma=False
    )
```

time: 427 us -> 102 us (0.24)
  waiting for transfers between devices: 348 us -> 0 us
  Pallas kernels: 0 us -> 99 us
  other arithmetic: 32.6 us -> 0 us
  matrix products: 26.7 us -> 0 us
  between operations: 13.3 us -> 0.01 us
    reduce_scatter x3 -> x0, waiting for transfers between devices: 343 us -> none  [the longest x1 177 us: on_device(): lax.psum_scatter(features_term(output_weight, mixed), 'wide', scatter_dim...]
    pallas_call x0 -> x1, Pallas kernels: none -> 99 us  [on_device(): pl.pallas_call(functools.partial(block_kernel, devices, length, rows_y),...]
    convert_element_type x3 -> x0, other arithmetic: 27.6 us -> none  [dequantize(): return (values.astype(jnp.float32) * expanded).astype(jnp.bfloat16)]
    dot_general x5 -> x0, matrix products: 26.2 us -> none  [the longest x3 24.8 us: features_term(): lax.dot_general(weight, activ, (((0,), (1,)), ((), ())), preferred_elemen...]
    all_gather x1 -> x0, waiting for transfers between devices: 4.85 us -> none  [on_device(): pair_all = lax.all_gather(pair_part, 'wide', axis=0, tiled=True)]
  transfers between devices with their start and end apart: 4 -> 0, of which waited for: 4 -> 0; matrix products, arithmetic and copies ran while one was open for 8% -> 0% of each run, Pallas kernels for 0% -> 0%
where the time goes in v1:
time: 102 us; the launch traced here: 101 us
  Pallas kernels  99 us (97%)
  local copies, waits for them, and re-layouts  1.87 us (2%)
    pallas_call x1, Pallas kernels, on_device(): pl.pallas_call(functools.partial(block_kernel, devices, length, rows_y),...  99 us

profile of v1, /device:TPU:10, one launch (start us, length us, event | category | flops | bytes accessed | tf_op | source)
XLA Modules:
  0.0 100.9 jit_solution(611094364806219689)
XLA Ops:
  0.0 99.0 %shard_map.100 = bf16[256,1024]{1,0:T(8,128)(2,1)} custom-call(bf16[256,1024]{1,0:T(8,128)(2,1)} %hidden.1, bf16[1024,8192]{1,0:T(8,128)(2,1)} %query_values.1, f32[64,8192]{1,0:T(8,128)} %query_scales.1, bf16[1024,1024]{1,0:T(8,128)(2,1)} %pair_values.1, f32[64,1024]{1,0:T(8,128)} %pair_scales.1, bf16[512,16384]{1,0:T(8,128)(2,1)} %output_values.1, ...), custom_call_target="tpu_custom_call" | custom-call | flops 9126805504 | bytes 35651584 | tf_op jit(solution)/shard_map/pallas_call | solution.py:411
  99.0 1.9 %copy.12 = bf16[256,1024]{1,0:T(8,128)(2,1)} copy(bf16[256,1024]{1,0:T(8,128)(2,1)} %shard_map.100) | data formatting | bytes 1048576

commit v2 on v1

--- a/solution.py
+++ b/solution.py
@@ -64,10 +64,10 @@
     tiles, tile_scales, tile_sem, tile_scales_sem, dequantized, acc,
     pair_buf, pair_scales_buf, pair_sem, kv_part,
     out_weight, out_scales, out_sem,
-    a_send, a_recv, a_ysend, a_yrecv, a_own, a_up, a_down,
-    a_ss, a_sr, a_ys, a_yr, a_zs, a_ur, a_dr,
-    b_send, b_recv, b_ysend, b_yrecv, b_own, b_up, b_down,
-    b_ss, b_sr, b_ys, b_yr, b_zs, b_ur, b_dr,
+    a_send, a_recv, a_ysend, a_yrecv, a_own, a_zrecv,
+    a_ss, a_sr, a_ys, a_yr, a_zs, a_zr,
+    b_send, b_recv, b_ysend, b_yrecv, b_own, b_zrecv,
+    b_ss, b_sr, b_ys, b_yr, b_zs, b_zr,
     kv_all, kv_send_sem, kv_recv_sem, keys, values, mixed,
 ):
     tokens, depth = hidden.shape
@@ -140,13 +140,8 @@
     for i in range(1, sharers):
         greet(me - share + rem(share + i, sharers))
 
-    @pl.when(z > 0)
-    def _():
-        greet(me - stride)
-
-    @pl.when(z < length - 1)
-    def _():
-        greet(me + stride)
+    for i in range(1, length):
+        greet(me + (rem(z + i, length) - z) * stride)
 
     def dequantize(source, scales, target, count, column, width, wide_column):
         for r in range(count):
@@ -168,9 +163,7 @@
         kv_part[head, :, into] = product[:, :HEAD_DIM]
         kv_part[head + 1, :, into] = product[:, HEAD_DIM:]
 
-    pl.semaphore_wait(
-        barrier, sharers - 1 + jnp.minimum(z, 1) + jnp.minimum(length - 1 - z, 1)
-    )
+    pl.semaphore_wait(barrier, sharers + length - 2)
 
     def remote(source, target, send_sem, recv_sem, device):
         return pltpu.make_async_remote_copy(
@@ -178,9 +171,23 @@
             device_id={"wide": device}, device_id_type=MESH,
         )
 
-    def reduce_scatter(multiply, rows, width, between, bufs):
-        send, recv, ysend, yrecv, own, up, down, ss, sr, ys, yr, zs, ur, dr = bufs
+    def reduce_scatter(multiply, below, width, between, bufs):
+        send, recv, ysend, yrecv, own, zrecv, ss, sr, ys, yr, zs, zr = bufs
+        rows = tokens + below
         block = acc.at[pl.ds(0, rows), pl.ds(0, width)]
+
+        def pack(target, value):
+            high = value.astype(BF16)
+            target[:rows, :] = high
+            if below:
+                target[rows:, :] = (value[tokens:] - high[tokens:].astype(F32)).astype(BF16)
+
+        def unpack(source):
+            top = source[:tokens, :].astype(F32)
+            if not below:
+                return top
+            low = source[tokens:rows, :].astype(F32) + source[rows:, :].astype(F32)
+            return jnp.concatenate([top, low], axis=0)
 
         def to_sibling(k):
             slot = rem(k, SIBLING_SLOTS)
@@ -200,7 +207,7 @@
                 def _():
                     to_sibling(k - SIBLING_SLOTS).wait_send()
 
-                send[rem(k, SIBLING_SLOTS)] = block[...].astype(BF16)
+                send[rem(k, SIBLING_SLOTS)] = block[...].astype(send.dtype)
                 to_sibling(k).start()
 
             @pl.when(for_sibling == 0)
@@ -209,7 +216,7 @@
                 if rows_y == 2:
                     @pl.when(k < length)
                     def _():
-                        ysend[k] = (block[...] + recv[k].astype(F32)).astype(BF16)
+                        pack(ysend.at[k], block[...] + recv[k].astype(F32))
                         to_across(k).start()
 
                     @pl.when(k >= length)
@@ -221,55 +228,34 @@
         for k in range(cells - SIBLING_SLOTS, cells):
             to_sibling(k).wait_send()
 
-        def to_up(j, zt):
-            return remote(yrecv.at[j], up.at[zt], zs.at[j], ur.at[zt], me + stride)
-
-        def to_down(j, zt):
-            return remote(yrecv.at[j], down.at[zt], zs.at[j], dr.at[zt], me - stride)
-
-        def collect(j):
+        def to_line(j, zt):
+            return remote(yrecv.at[j], zrecv.at[z], zs.at[j], zr.at[z], me + (zt - z) * stride)
+
+        def from_line(zf):
+            return remote(yrecv.at[0], zrecv.at[zf], zs.at[0], zr.at[zf], me + (zf - z) * stride)
+
+        def collected(j):
             if rows_y == 2:
                 to_across(j).wait_recv()
-                own[j] = own[j] + yrecv[j].astype(F32)
-
-        def from_below(j, zt):
-            @pl.when(z > 0)
-            def _():
-                to_up(0, zt).wait_recv()
-                own[j] = own[j] + up[zt].astype(F32)
-
-        def from_above(j, zt):
-            @pl.when(z < length - 1)
-            def _():
-                to_down(0, zt).wait_recv()
-                own[j] = own[j] + down[zt].astype(F32)
+                return own[j] + unpack(yrecv.at[j])
+            return own[j]
 
         @pl.loop(0, length - 1)
         def _(j):
             between(j)
-            zt = line_order(z, length, j)
-            collect(j)
-
-            @pl.when(zt > z)
-            def _():
-                from_below(j, zt)
-                yrecv[j] = own[j].astype(BF16)
-                to_up(j, zt).start()
-
-            @pl.when(zt < z)
-            def _():
-                from_above(j, zt)
-                yrecv[j] = own[j].astype(BF16)
-                to_down(j, zt).start()
+            pack(yrecv.at[j], collected(j))
+            to_line(j, line_order(z, length, j)).start()
 
         between(length - 1)
-        collect(length - 1)
-        from_below(length - 1, z)
-        from_above(length - 1, z)
+        own[length - 1] = collected(length - 1)
+        for i in range(1, length):
+            zf = rem(z + i, length)
+            from_line(zf).wait_recv()
+            own[length - 1] = own[length - 1] + unpack(zrecv.at[zf])
 
         def settle():
             for j in range(length - 1):
-                to_up(j, z).wait_send()
+                to_line(j, line_order(z, length, jnp.int32(j))).wait_send()
             if rows_y == 2:
                 for j in range(length):
                     to_across(j).wait_send()
@@ -308,8 +294,8 @@
             dequantize(out_weight, out_scales, out_weight, depth_b // 16, column, 512, column)
 
     total, settle_a = reduce_scatter(
-        multiply_a, tokens + extra, block_a, prepare_output,
-        (a_send, a_recv, a_ysend, a_yrecv, a_own, a_up, a_down, a_ss, a_sr, a_ys, a_yr, a_zs, a_ur, a_dr),
+        multiply_a, extra, block_a, prepare_output,
+        (a_send, a_recv, a_ysend, a_yrecv, a_own, a_zrecv, a_ss, a_sr, a_ys, a_yr, a_zs, a_zr),
     )
 
     def to_sharer(i):
@@ -369,8 +355,8 @@
         acc[:tokens, :block_b] = jnp.dot(mixed[...], out_weight[:, columns], preferred_element_type=F32)
 
     summed, settle_b = reduce_scatter(
-        multiply_b, tokens, block_b, lambda j: None,
-        (b_send, b_recv, b_ysend, b_yrecv, b_own, b_up, b_down, b_ss, b_sr, b_ys, b_yr, b_zs, b_ur, b_dr),
+        multiply_b, 0, block_b, lambda j: None,
+        (b_send, b_recv, b_ysend, b_yrecv, b_own, b_zrecv, b_ss, b_sr, b_ys, b_yr, b_zs, b_zr),
     )
     out[...] = (summed[...] * tensor_scales[3]).astype(BF16)
     settle_b()
@@ -391,18 +377,17 @@
     cosine, sine = rotary_tables(tokens)
     dma = pltpu.SemaphoreType.DMA
 
-    def buffers(rows, width):
-        slots_y = length if rows_y == 2 else 1
+    def buffers(below, width, sibling_type):
+        rows, wire = tokens + below, tokens + 2 * below
         return [
-            pltpu.VMEM((SIBLING_SLOTS, rows, width), BF16),
-            pltpu.VMEM((cells, rows, width), BF16),
-            pltpu.VMEM((slots_y, rows, width) if rows_y == 2 else (1, 16, 128), BF16),
-            pltpu.VMEM((length, rows, width), BF16),
+            pltpu.VMEM((SIBLING_SLOTS, rows, width), sibling_type),
+            pltpu.VMEM((cells, rows, width), sibling_type),
+            pltpu.VMEM((length, wire, width) if rows_y == 2 else (1, 16, 128), BF16),
+            pltpu.VMEM((length, wire, width), BF16),
             pltpu.VMEM((length, rows, width), F32),
-            pltpu.VMEM((length, rows, width), BF16),
-            pltpu.VMEM((length, rows, width), BF16),
+            pltpu.VMEM((length, wire, width), BF16),
             dma((SIBLING_SLOTS,)), dma((cells,)), dma((length,)), dma((length,)),
-            dma((length,)), dma((length,)), dma((length,)),
+            dma((length,)), dma((length,)),
         ]
 
     anywhere = pl.BlockSpec(memory_space=pl.ANY)
@@ -427,8 +412,8 @@
             pltpu.VMEM(output_scales.shape, F32),
             dma((2, length)),
         ]
-        + buffers(tokens + extra, block_a)
-        + buffers(tokens, block_b)
+        + buffers(extra, block_a, F32)
+        + buffers(0, block_b, BF16)
         + [
             pltpu.VMEM((sharers, extra, block_a), F32),
             dma((sharers,)), dma((sharers,)),

time: 102 us -> 112 us (1.098)
  Pallas kernels: 99 us -> 110 us
    pallas_call x1, Pallas kernels: 99 us -> 110 us  [on_device(): pl.pallas_call(functools.partial(block_kernel, devices, length, rows_y),...]
where the time goes in v2:
time: 112 us
  Pallas kernels  110 us (98%)
  local copies, waits for them, and re-layouts  1.87 us (2%)
    pallas_call x1, Pallas kernels, on_device(): pl.pallas_call(functools.partial(block_kernel, devices, length, rows_y),...  110 us

profile of v2, /device:TPU:10, one launch (start us, length us, event | category | flops | bytes accessed | tf_op | source)
XLA Modules:
  0.0 111.8 jit_solution(3059492636452675749)
XLA Ops:
  0.0 109.9 %shard_map.100 = bf16[256,1024]{1,0:T(8,128)(2,1)} custom-call(bf16[256,1024]{1,0:T(8,128)(2,1)} %hidden.1, bf16[1024,8192]{1,0:T(8,128)(2,1)} %query_values.1, f32[64,8192]{1,0:T(8,128)} %query_scales.1, bf16[1024,1024]{1,0:T(8,128)(2,1)} %pair_values.1, f32[64,1024]{1,0:T(8,128)} %pair_scales.1, bf16[512,16384]{1,0:T(8,128)(2,1)} %output_values.1, ...), custom_call_target="tpu_custom_call" | custom-call | flops 9126805504 | bytes 35651584 | tf_op jit(solution)/shard_map/pallas_call | solution.py:396
  109.9 1.9 %copy.12 = bf16[256,1024]{1,0:T(8,128)(2,1)} copy(bf16[256,1024]{1,0:T(8,128)(2,1)} %shard_map.100) | data formatting | bytes 1048576

commit v3 on v2

--- a/solution.py
+++ b/solution.py
@@ -228,11 +228,26 @@
         for k in range(cells - SIBLING_SLOTS, cells):
             to_sibling(k).wait_send()
 
-        def to_line(j, zt):
-            return remote(yrecv.at[j], zrecv.at[z], zs.at[j], zr.at[z], me + (zt - z) * stride)
-
-        def from_line(zf):
-            return remote(yrecv.at[0], zrecv.at[zf], zs.at[0], zr.at[zf], me + (zf - z) * stride)
+        def to_up(j, zt):
+            return remote(yrecv.at[j], zrecv.at[zt], zs.at[j], zr.at[zt], me + stride)
+
+        def to_down(j, zt):
+            slot = zt + (1 - jnp.minimum(z - 1 - zt, 1)) * (length - zt)
+            return remote(yrecv.at[j], zrecv.at[slot], zs.at[j], zr.at[slot], me - stride)
+
+        def add_arrived(j, slot, device):
+            remote(yrecv.at[0], zrecv.at[slot], zs.at[0], zr.at[slot], device).wait_recv()
+            own[j] = own[j] + unpack(zrecv.at[slot])
+
+        def from_below(j, zt):
+            @pl.when(z > 0)
+            def _():
+                add_arrived(j, zt, me - stride)
+
+        def from_above(j, slot):
+            @pl.when(z < length - 1)
+            def _():
+                add_arrived(j, slot, me + stride)
 
         def collected(j):
             if rows_y == 2:
@@ -243,19 +258,29 @@
         @pl.loop(0, length - 1)
         def _(j):
             between(j)
-            pack(yrecv.at[j], collected(j))
-            to_line(j, line_order(z, length, j)).start()
+            zt = line_order(z, length, j)
+            own[j] = collected(j)
+
+            @pl.when(zt > z)
+            def _():
+                from_below(j, zt)
+                pack(yrecv.at[j], own[j])
+                to_up(j, zt).start()
+
+            @pl.when(zt < z)
+            def _():
+                from_above(j, zt)
+                pack(yrecv.at[j], own[j])
+                to_down(j, zt).start()
 
         between(length - 1)
         own[length - 1] = collected(length - 1)
-        for i in range(1, length):
-            zf = rem(z + i, length)
-            from_line(zf).wait_recv()
-            own[length - 1] = own[length - 1] + unpack(zrecv.at[zf])
+        from_below(length - 1, z)
+        from_above(length - 1, length)
 
         def settle():
             for j in range(length - 1):
-                to_line(j, line_order(z, length, jnp.int32(j))).wait_send()
+                to_up(j, z).wait_send()
             if rows_y == 2:
                 for j in range(length):
                     to_across(j).wait_send()
@@ -385,9 +410,9 @@
             pltpu.VMEM((length, wire, width) if rows_y == 2 else (1, 16, 128), BF16),
             pltpu.VMEM((length, wire, width), BF16),
             pltpu.VMEM((length, rows, width), F32),
-            pltpu.VMEM((length, wire, width), BF16),
+            pltpu.VMEM((length + 1, wire, width), BF16),
             dma((SIBLING_SLOTS,)), dma((cells,)), dma((length,)), dma((length,)),
-            dma((length,)), dma((length,)),
+            dma((length,)), dma((length + 1,)),
         ]
 
     anywhere = pl.BlockSpec(memory_space=pl.ANY)

time: 112 us -> 104 us (0.929)
  Pallas kernels: 110 us -> 102 us
    pallas_call x1, Pallas kernels: 110 us -> 102 us  [on_device(): pl.pallas_call(functools.partial(block_kernel, devices, length, rows_y),...]
where the time goes in v3:
time: 104 us
  Pallas kernels  102 us (98%)
  local copies, waits for them, and re-layouts  1.87 us (2%)
    pallas_call x1, Pallas kernels, on_device(): pl.pallas_call(functools.partial(block_kernel, devices, length, rows_y),...  102 us

profile of v3, /device:TPU:10, one launch (start us, length us, event | category | flops | bytes accessed | tf_op | source)
XLA Modules:
  0.0 103.6 jit_solution(7861969338717947127)
XLA Ops:
  0.0 101.7 %shard_map.100 = bf16[256,1024]{1,0:T(8,128)(2,1)} custom-call(bf16[256,1024]{1,0:T(8,128)(2,1)} %hidden.1, bf16[1024,8192]{1,0:T(8,128)(2,1)} %query_values.1, f32[64,8192]{1,0:T(8,128)} %query_scales.1, bf16[1024,1024]{1,0:T(8,128)(2,1)} %pair_values.1, f32[64,1024]{1,0:T(8,128)} %pair_scales.1, bf16[512,16384]{1,0:T(8,128)(2,1)} %output_values.1, ...), custom_call_target="tpu_custom_call" | custom-call | flops 9126805504 | bytes 35651584 | tf_op jit(solution)/shard_map/pallas_call | solution.py:421
  101.7 1.9 %copy.12 = bf16[256,1024]{1,0:T(8,128)(2,1)} copy(bf16[256,1024]{1,0:T(8,128)(2,1)} %shard_map.100) | data formatting | bytes 1048576
